TPU v7x, 256 devices: a whole 4x4x8 slice. The times are simulated.
256 devices in a mesh: ctx: 16 (over y_lo, z), head: 16 (over x, y_hi, core).
Axes of the slice: x: 4, y: 4 (y_hi: 2, y_lo: 2; y = y_hi * 2 + y_lo), z: 8, core: 2. Of those that a mesh axis runs over, the one named last changes fastest.
Arguments:
- q_noisy: bfloat16 [8192, 2048], P('ctx', 'head'), may hold values from -8 to 8
- k_noisy: bfloat16 [8192, 2048], P('ctx', 'head'), may hold values from -8 to 8
- v_noisy: bfloat16 [8192, 2048], P('ctx', 'head'), may hold values from -8 to 8
- k_clean: bfloat16 [8192, 2048], P('ctx', 'head'), may hold values from -8 to 8
- v_clean: bfloat16 [8192, 2048], P('ctx', 'head'), may hold values from -8 to 8
- out_weight: bfloat16 [2048, 4096], P('head'), may hold values from -0.1875 to 0.1875
- cotangent: bfloat16 [8192, 4096], P('ctx', 'head'), may hold values from -6 to 6
- noise_mask: int32 [8192], P('ctx'), may hold values from 0 to 1, as said below
- block_order: int32 [32], replicated, may hold values from 0 to 31, as said below
Outputs:
- mixed: bfloat16 [8192, 4096], P('ctx', 'head')
- grad_q_noisy: bfloat16 [8192, 2048], P('ctx', 'head')
- grad_k_noisy: bfloat16 [8192, 2048], P('ctx', 'head')
- grad_v_noisy: bfloat16 [8192, 2048], P('ctx', 'head')
- grad_k_clean: bfloat16 [8192, 2048], P('ctx', 'head')
- grad_v_clean: bfloat16 [8192, 2048], P('ctx', 'head')
- grad_out_weight: float32 [2048, 4096], P('head', 'ctx')
Inputs may be any that keep to these rules, and one draw needn't show every extreme that they name: `noise_mask`: each block of 256 rows has its own share of ones. `block_order`: A permutation of the 32 block numbers; stored blocks 2j and 2j + 1 hold numbers that add up to 31.
All inputs are finite; a program needn't handle non-finite values.
Results may differ from a plain program's by a relative error of at most 0.04.
Values may be sent and summed in bfloat16 or wider, within the bound.
A program may use at most 128 MiB of HBM per device.

v0:
```python
import functools

import jax
import jax.numpy as jnp
from jax import lax
from jax.experimental import pallas as pl
from jax.experimental.pallas import tpu as pltpu
from jax.sharding import PartitionSpec as P

BLOCK = 256
HEAD_DIM = 128
SCALE = HEAD_DIM**-0.5
SCALE2 = SCALE * 1.4426950408889634
EMPTY = -1e30
NZ = 8
MESH = pl.DeviceIdType.MESH
BF = jnp.bfloat16
F32 = jnp.float32


def nt(a, b):
    return lax.dot_general(a, b, (((1,), (1,)), ((), ())), preferred_element_type=F32)


def nn(a, b):
    return lax.dot_general(a, b, (((1,), (0,)), ((), ())), preferred_element_type=F32)


def remote(src, dst, send_sem, recv_sem, device):
    return pltpu.make_async_remote_copy(
        src_ref=src,
        dst_ref=dst,
        send_sem=send_sem,
        recv_sem=recv_sem,
        device_id=device,
        device_id_type=MESH,
    )


def forward_tile(keys, values_t, queries, state):
    row_max, row_sum, acc = state
    scores = nt(keys, queries)
    new_max = jnp.maximum(row_max, jnp.max(scores, axis=0, keepdims=True))
    weights = jnp.exp2((scores - new_max) * SCALE2)
    shrink = jnp.exp2((row_max - new_max) * SCALE2)
    new_sum = row_sum * shrink + jnp.sum(weights, axis=0, keepdims=True)
    new_acc = acc * shrink + nn(values_t, weights.astype(BF))
    return new_max, new_sum, new_acc


def backward_tile(keys, values, keys_t, queries, grads, log_total, row_dot):
    probs = jnp.exp2(nt(keys, queries) * SCALE2 - log_total)
    grad_probs = nt(values, grads)
    grad_scores = (probs * (grad_probs - row_dot)).astype(BF)
    return nn(grad_scores, queries), nn(probs.astype(BF), grads), nn(keys_t, grad_scores)


def kernel(
    order, mask, q_in, kn_in, vn_in, kc_in, vc_in, w_in, cot_in,
    mixed, gq, gkn, gvn, gkc, gvc, gw,
    q, kn, vn, kc, vc, w, cot,
    qs, kns, vns, kv, kt, vt, knt, vnt, ml, ml_in, acc, acc_out, acc_in,
    cotm, cot_all, w_cols, w_mid, att_t, att_all, do_acc, dos, ld, dq, dq_out, dq_in,
    cb, rs_out, rs_in, gy_out, gy_in, g_out, g_in, stage, finals, mixed_final, gw_final,
    in_sem, out_sem,
    kv_ss, kv_rs, y_ss, y_rs, gy_ss, gy_rs, c_ss, c_rs, a_ss, a_rs, wm_ss, wm_rs, w_ss, w_rs,
    r_ss, r_rs, g_ss, g_rs,
):
    c = lax.axis_index("ctx")
    h = lax.axis_index("head")
    yl, z = c // NZ, c % NZ
    x, yh, co = h // 4, (h // 2) % 2, h % 2
    sends = []

    def go(copy):
        copy.start()
        sends.append(copy)

    def head_of(x_, yh_, co_):
        return x_ * 4 + yh_ * 2 + co_

    z_dev = [(yl * NZ + (z + 1) % NZ, h), (yl * NZ + (z + NZ - 1) % NZ, h)]
    y_ctx = (1 - yl) * NZ + z
    y_dev = (y_ctx, h)
    heads = [head_of((x + k) % 4, yh, co_) for k in range(1, 4) for co_ in range(2)]
    heads += [head_of(x, yh, 1 - co), head_of(x, 1 - yh, co)]

    loads = [
        pltpu.make_async_copy(src, dst, in_sem.at[i])
        for i, (src, dst) in enumerate(
            ((kc_in, kc), (vc_in, vc), (cot_in, cot), (q_in, q), (kn_in, kn), (vn_in, vn), (w_in, w))
        )
    ]
    for load in loads:
        load.start()
    stores = []

    def put(src, dst):
        store = pltpu.make_async_copy(src, dst, out_sem.at[len(stores)])
        store.start()
        stores.append(store)

    barrier = pltpu.get_barrier_semaphore()
    for dev in z_dev + [y_dev] + [(c, p) for p in heads]:
        pl.semaphore_signal(barrier, inc=1, device_id=dev, device_id_type=MESH)

    swap = order[2 * c] > order[2 * c + 1]

    def in_order(ref, i):
        first, second = ref[:BLOCK, :], ref[BLOCK:, :]
        return jnp.where(swap, first, second) if i else jnp.where(swap, second, first)

    def low_id(ctx):
        return jnp.minimum(order[2 * ctx], order[2 * ctx + 1])

    loads[0].wait()
    loads[1].wait()
    for i in range(2):
        kv[z, 0, i] = in_order(kc, i)
        kv[z, 1, i] = in_order(vc, i)
    loads[2].wait()
    row_id = lax.broadcasted_iota(jnp.int32, (128, 128), 0)
    col_id = lax.broadcasted_iota(jnp.int32, (128, 128), 1)
    for b in range(4):
        flags = jnp.broadcast_to(mask[b : b + 1, :].astype(F32), (128, 128))
        column = jnp.sum(jnp.where(row_id == col_id, flags, 0.0), axis=1, keepdims=True)
        rows = slice(b * 128, (b + 1) * 128)
        cotm[rows, :] = (cot[rows, :].astype(F32) * column).astype(BF)
    for i in range(2):
        cot_all[h, i * BLOCK : (i + 1) * BLOCK, :] = in_order(cotm, i)

    loads[3].wait()
    for i in range(2):
        qs[0, i] = in_order(q, i)

    pl.semaphore_wait(barrier, 11)

    def kv_chunk(d, s, t, i, slot):
        chunk = kv.at[slot, t, i]
        return remote(chunk, chunk, kv_ss.at[d, s - 1, t, i], kv_rs.at[d, s - 1, t, i], z_dev[d])

    def kv_copy(d, s, t, i):
        return kv_chunk(d, s, t, i, (z + NZ - (s - 1)) % NZ if d == 0 else (z + s - 1) % NZ)

    def kv_wait(d, s, t, i):
        kv_chunk(d, s, t, i, (z + NZ - s) % NZ if d == 0 else (z + s) % NZ).wait_recv()

    def head_copy(buf, ss, rs, index, slot, dev_head):
        return remote(buf.at[slot], buf.at[slot], ss.at[index], rs.at[index], (c, dev_head))

    yh_head = head_of(x, 1 - yh, co)
    sib = head_of(x, yh, 1 - co)

    def x_head(k, yh_, co_):
        return head_of((x + k) % 4, yh_, co_)

    def rows_at(half):
        return pl.ds(BLOCK * half, BLOCK)

    def yh_copy(buf, ss, rs, half, slot):
        chunk = buf.at[slot, rows_at(half)]
        return remote(chunk, chunk, ss.at[half], rs.at[half], (c, yh_head))

    def x_copy(buf, ss, rs, second, d, kind, slot):
        index = 2 + 6 * second + 2 * kind + d
        chunk = buf.at[slot, rows_at(d if kind == 2 else kind)]
        dev = (c, x_head(1 if d == 0 else 3, yh, co))
        return remote(chunk, chunk, ss.at[index], rs.at[index], dev)

    def near_slot(second, d):
        return x_head(3 if d == 0 else 1, 1 - yh if second else yh, co)

    def gather_begin(buf, ss, rs, between=lambda: None):
        for half in range(2):
            go(yh_copy(buf, ss, rs, half, h))
            for d in range(2):
                go(x_copy(buf, ss, rs, 0, d, half, h))
            if half == 0:
                between()
        go(head_copy(buf, ss, rs, 14, h, sib))

    def gather_second(buf, ss, rs, half):
        yh_copy(buf, ss, rs, half, yh_head).wait_recv()
        for d in range(2):
            go(x_copy(buf, ss, rs, 1, d, half, yh_head))
        if half:
            go(head_copy(buf, ss, rs, 15, yh_head, sib))

    def gather_pass(buf, ss, rs, second, d):
        slot = near_slot(second, d)
        x_copy(buf, ss, rs, second, d, d, slot).wait_recv()
        go(x_copy(buf, ss, rs, second, d, 2, slot))

    def gather_near(buf, ss, rs, second):
        for d in range(2):
            slot = near_slot(second, d)
            x_copy(buf, ss, rs, second, d, 1 - d, slot).wait_recv()
            go(head_copy(buf, ss, rs, 16 + 2 * second + d, slot, sib))

    def gather_far(buf, ss, rs, second):
        slot = x_head(2, 1 - yh if second else yh, co)
        for d in range(2):
            x_copy(buf, ss, rs, second, d, 2, slot).wait_recv()
        go(head_copy(buf, ss, rs, 20 + second, slot, sib))

    def gather_end(buf, ss, rs):
        slots = [sib, x_head(0, 1 - yh, 1 - co)]
        for yh_ in (yh, 1 - yh):
            slots += [x_head(3, yh_, 1 - co), x_head(1, yh_, 1 - co)]
        slots += [x_head(2, yh_, 1 - co) for yh_ in (yh, 1 - yh)]
        for j, slot in enumerate(slots):
            head_copy(buf, ss, rs, 14 + j, slot, sib).wait_recv()

    def y_copy(index, src, dst):
        return remote(src, dst, y_ss.at[index], y_rs.at[index], y_dev)

    for t in range(2):
        for i in range(2):
            for d in range(2):
                go(kv_copy(d, 1, t, i))
    q_copy = y_copy(0, qs.at[0], qs.at[1])
    gather_begin(cot_all, c_ss, c_rs, lambda: go(q_copy))

    loads[4].wait()
    loads[5].wait()
    for i in range(2):
        kns[i] = in_order(kn, i)
        vns[i] = in_order(vn, i)
        knt[i] = kns[i].T
        vnt[i] = vns[i].T

    def transpose_slot(slot):
        for i in range(2):
            kt[slot, i] = kv[slot, 0, i].T
            vt[slot, i] = kv[slot, 1, i].T

    def get_state(qd, i):
        return ml[qd, i], ml[qd, 2 + i], acc[qd, i]

    def put_state(qd, i, state):
        ml[qd, i], ml[qd, 2 + i] = (jnp.broadcast_to(v, (8, BLOCK)) for v in state[:2])
        acc[qd, i] = state[2]

    def rows_of(state):
        return state[0][:1], state[1][:1], state[2]

    def seen_high(qd, slot):
        q_ctx = (yl + qd * (1 - 2 * yl)) * NZ + z
        return low_id(yl * NZ + slot) > low_id(q_ctx)

    def forward_pair(qd, slot):
        high = seen_high(qd, slot)
        q_low, q_high = qs[qd, 0], qs[qd, 1]
        state_high = forward_tile(
            kv[slot, 0, 0], vt[slot, 0], q_high, rows_of(get_state(qd, 1))
        )
        state_low = rows_of(get_state(qd, 0))
        state = tuple(jnp.where(high, a, b) for a, b in zip(state_high, state_low))
        state = forward_tile(
            jnp.where(high, kv[slot, 0, 1], kv[slot, 0, 0]),
            jnp.where(high, vt[slot, 1], vt[slot, 0]),
            jnp.where(high, q_high, q_low),
            state,
        )
        put_state(qd, 0, tuple(jnp.where(high, b, a) for a, b in zip(state, state_low)))
        put_state(qd, 1, tuple(jnp.where(high, a, b) for a, b in zip(state, state_high)))

    def w_across(j):
        columns = pl.ds(pl.multiple_of((j * 4 + (1 - yh) * 2) * 256, 512), 512)
        return remote(w.at[:, columns], w_mid.at[j], wm_ss.at[j], wm_rs.at[j], (c, yh_head))

    def send_w_across():
        loads[6].wait()
        for j in range(4):
            go(w_across(j))

    w_steps = [(1, 0), (1, 1), (3, 0), (3, 1), (2, 0), (2, 1), (0, 1)]

    def send_w(passed):
        if passed:
            for j in range(4):
                w_across(j).wait_recv()
        slot = yh_head if passed else h
        for j, (k, other) in enumerate(w_steps + [(0, 0)]):
            dest_core = (1 - co) if other else co
            if passed:
                columns = pl.ds(pl.multiple_of(dest_core * 256, 256), 256)
                src = w_mid.at[(x + k) % 4, :, columns]
            else:
                first = pl.multiple_of(head_of((x + k) % 4, yh, dest_core) * 256, 256)
                src = w.at[:, pl.ds(first, 256)]
            if j < 7:
                index = 7 * passed + j
                dev = (c, head_of((x + k) % 4, yh, dest_core))
                go(remote(src, w_cols.at[slot], w_ss.at[index], w_rs.at[index], dev))
            else:
                w_cols[slot] = src[...]

    def wait_w():
        for passed in range(2):
            for j, (k, other) in enumerate(w_steps):
                core = (1 - co) if other else co
                slot = head_of((x + 4 - k) % 4, 1 - yh if passed else yh, core)
                index = 7 * passed + j
                dev = (c, head_of((x + k) % 4, yh, core))
                here = w_cols.at[slot]
                remote(here, here, w_ss.at[index], w_rs.at[index], dev).wait_recv()

    def add_pieces(core, first):
        for i in range(2):
            rows = slice(i * BLOCK, (i + 1) * BLOCK)
            total = jnp.zeros((BLOCK, HEAD_DIM), F32) if first else do_acc[rows, :]
            for j in range(8):
                p = 2 * j + core
                columns = pl.ds(pl.multiple_of(p * 256, 256), 256)
                total = total + nt(cot_all[p, rows], w[:, columns])
            do_acc[rows, :] = total

    empty = (
        jnp.full((1, BLOCK), EMPTY, F32),
        jnp.zeros((1, BLOCK), F32),
        jnp.zeros((HEAD_DIM, BLOCK), F32),
    )
    transpose_slot(z)
    for i in range(2):
        state = forward_tile(kns[i], vnt[i], qs[0, i], empty)
        if i == 1:
            state = forward_tile(kv[z, 0, 0], vt[z, 0], qs[0, 1], state)
        put_state(0, i, state)
        put_state(1, i, empty)
    def slot_tasks(slot):
        def first():
            transpose_slot(slot)
            forward_pair(0, slot)

        return [first, lambda: forward_pair(1, slot)]

    def late_queries():
        q_copy.wait_recv()
        forward_pair(1, z)

    cot_args = (cot_all, c_ss, c_rs)
    hooks = {
        (1, 2): lambda: gather_second(*cot_args, 0),
        (1, 3): lambda: [gather_pass(*cot_args, 0, d) for d in range(2)],
        (2, 1): lambda: [gather_second(*cot_args, 1), gather_near(*cot_args, 0)],
        (2, 2): lambda: gather_pass(*cot_args, 1, 0),
        (2, 3): lambda: send_w_across(),
        (3, 0): lambda: gather_far(*cot_args, 0),
        (3, 1): lambda: gather_pass(*cot_args, 1, 1),
        (3, 3): lambda: gather_near(*cot_args, 1),
    }
    tasks = []
    for s in range(1, 5):
        events = [(t, i) for t in range(2) for i in range(2)]
        if s == 4:
            events = [(t, i) for i in range(2) for t in range(2)]
        for n, (t, i) in enumerate(events):
            for d in range(2):
                if s < 4 or t == d:
                    kv_wait(d, s, t, i)
                    if s < 3 or (s == 3 and t == d):
                        go(kv_copy(d, s + 1, t, i))
            if (s, n) in hooks:
                hooks[s, n]()
            if tasks:
                tasks.pop(0)()
        if s == 1:
            tasks.append(late_queries)
        if s < 4:
            tasks += slot_tasks((z + NZ - s) % NZ) + slot_tasks((z + s) % NZ)
    while tasks:
        tasks.pop(0)()
    slot = (z + 4) % NZ
    transpose_slot(slot)
    forward_pair(1, slot)
    for i in range(2):
        acc_out[i] = acc[1, i].astype(BF)
    ml_copy = y_copy(1, ml.at[1], ml_in)
    acc_copy = y_copy(2, acc_out, acc_in)
    go(ml_copy)
    go(acc_copy)
    gather_far(*cot_args, 1)
    add_pieces(co, True)
    gather_end(*cot_args)
    add_pieces(1 - co, False)
    for i in range(2):
        dos[0, i] = do_acc[i * BLOCK : (i + 1) * BLOCK, :].astype(BF)
    do_copy = y_copy(3, dos.at[0], dos.at[1])
    go(do_copy)
    forward_pair(0, (z + 4) % NZ)
    send_w(0)

    ml_copy.wait_recv()
    acc_copy.wait_recv()
    for i in range(2):
        own_max, own_sum, own_acc = rows_of(get_state(0, i))
        other_max, other_sum = ml_in[i][:1], ml_in[2 + i][:1]
        top = jnp.maximum(own_max, other_max)
        own_part = jnp.exp2((own_max - top) * SCALE2)
        other_part = jnp.exp2((other_max - top) * SCALE2)
        total = own_sum * own_part + other_sum * other_part
        weighted = own_acc * own_part + acc_in[i].astype(F32) * other_part
        attended_t = (weighted / total).astype(BF)
        att_t[:, i * BLOCK : (i + 1) * BLOCK] = attended_t
        att_all[h, i * BLOCK : (i + 1) * BLOCK, :] = attended_t.T
        grads_t = dos[0, i].T.astype(F32)
        row_dot = jnp.sum(grads_t * attended_t.astype(F32), axis=0, keepdims=True)
        ld[0, i] = jnp.broadcast_to(top * SCALE2 + jnp.log2(total), (8, BLOCK))
        ld[0, 2 + i] = jnp.broadcast_to(row_dot, (8, BLOCK))
    ld_copy = y_copy(4, ld.at[0], ld.at[1])
    go(ld_copy)
    gather_begin(att_all, a_ss, a_rs)

    def gy_slot(j):
        return (z + (4, 3, 5, 2, 6, 1, 7, 0)[j]) % NZ

    gy_copies = []

    def send_gy(first, last):
        for j in range(first, last):
            slot = gy_slot(j)
            gy_out[j] = nn(att_t[...], cot_all[(1 - yl) * NZ + slot]).astype(BF)
            gy_copies.append(remote(gy_out.at[j], gy_in.at[j], gy_ss.at[j], gy_rs.at[j], y_dev))
            go(gy_copies[-1])

    send_gy(0, 3)

    for i in range(2):
        key_term, value_term, query_term = backward_tile(
            kns[i], vns[i], knt[i], qs[0, i], dos[0, i], ld[0, i][:1], ld[0, 2 + i][:1]
        )
        stage[0, i] = (key_term * SCALE).astype(BF)
        stage[1, i] = value_term.astype(BF)
        dq[0, i] = query_term
        dq[1, i] = jnp.zeros_like(query_term)

    def unsort(index, out):
        for b in range(2):
            rows = jnp.where(swap, stage[index, 1 - b], stage[index, b])
            finals[index, b * BLOCK : (b + 1) * BLOCK, :] = rows
        put(finals.at[index], out)

    unsort(0, gkn)
    unsort(1, gvn)

    def backward_pair(par, d, qd, slot, same=False):
        low, high = (
            backward_tile(
                kv[slot, 0, 0], kv[slot, 1, 0], kt[slot, 0],
                qs[qd, 1], dos[qd, 1], ld[qd, 1][:1], ld[qd, 3][:1],
            ),
            None,
        )
        if same:
            cb[par, d, 0, 0] = low[0]
            cb[par, d, 1, 0] = low[1]
            cb[par, d, 0, 1] = jnp.zeros_like(low[0])
            cb[par, d, 1, 1] = jnp.zeros_like(low[1])
            dq[qd, 1] += low[2]
            return
        pick = seen_high(qd, slot)

        def chosen(first, second):
            return jnp.where(pick, second, first)

        high = backward_tile(
            chosen(kv[slot, 0, 0], kv[slot, 0, 1]),
            chosen(kv[slot, 1, 0], kv[slot, 1, 1]),
            chosen(kt[slot, 0], kt[slot, 1]),
            chosen(qs[qd, 0], qs[qd, 1]),
            chosen(dos[qd, 0], dos[qd, 1]),
            chosen(ld[qd, 0][:1], ld[qd, 1][:1]),
            chosen(ld[qd, 2][:1], ld[qd, 3][:1]),
        )
        to_high = pick.astype(F32)
        to_low = 1.0 - to_high
        for t in range(2):
            new_low = low[t] + high[t] * to_low
            new_high = high[t] * to_high
            if qd == 0:
                cb[par, d, t, 0] = new_low
                cb[par, d, t, 1] = new_high
            else:
                cb[par, d, t, 0] += new_low
                cb[par, d, t, 1] += new_high
        dq[qd, 0] += high[2] * to_low
        dq[qd, 1] += low[2] + high[2] * to_high

    def contribution_tasks(s):
        par = s % 2
        if s in (0, 4):
            slot = (z + 4 - s) % NZ
            pairs = [(0, 0, slot, s == 4), (0, 1, slot)]
        else:
            slots = [(z + 4 - s) % NZ, (z + NZ - 4 + s) % NZ]
            pairs = [(d, qd, slots[d]) for d in range(2) for qd in range(2)]
        return [functools.partial(backward_pair, par, *pair) for pair in pairs]

    factors = (SCALE, 1.0)

    def rs_copy(d, s, t, i):
        at = (d, s, t, i)
        return remote(rs_out.at[at], rs_in.at[at], r_ss.at[at], r_rs.at[at], z_dev[d])

    def g_copy(d, s):
        rows = pl.ds(64 * d, 64) if s == 0 else pl.ds(0, 128)
        return remote(
            g_out.at[d, s, rows], g_in.at[d, s, rows], g_ss.at[d, s], g_rs.at[d, s], z_dev[d]
        )

    def g_piece(j):
        gy_copies[j].wait_recv()
        own = nn(att_t[...], cot_all[yl * NZ + gy_slot(j)])
        return own + gy_in[j].astype(F32)

    own, other = contribution_tasks(0)
    own()
    do_copy.wait_recv()
    ld_copy.wait_recv()
    other()
    for t in range(2):
        for i in range(2):
            rs_out[t, 0, t, i] = (cb[0, 0, t, i] * factors[t]).astype(BF)
            go(rs_copy(t, 0, t, i))
    send_gy(3, 8)
    send_w(1)

    def rs_step(s, tasks):
        for t, i, d in [(t, i, d) for t in range(2) for i in range(2) for d in range(2)]:
            term = cb[s % 2, d, t, i] * factors[t]
            if s > 1 or t == d:
                rs_copy(d, s - 1, t, i).wait_recv()
                term = term + rs_in[d, s - 1, t, i].astype(F32)
            rs_out[d, s, t, i] = term.astype(BF)
            go(rs_copy(d, s, t, i))
            if d and tasks:
                tasks.pop(0)()

    def g_step(s):
        if s == 0:
            piece = g_piece(0).astype(BF)
            for d in range(2):
                g_out[d, 0] = piece
                go(g_copy(d, 0))
            return
        for d in range(2):
            piece = g_piece(2 * s - 1 + d)
            g_copy(d, s - 1).wait_recv()
            if s == 1:
                half = slice(64 * d, 64 * d + 64)
                rest = slice(64 - 64 * d, 128 - 64 * d)
                g_out[d, 1, half] = (piece[half] + g_in[d, 0, half].astype(F32)).astype(BF)
                g_out[d, 1, rest] = piece[rest].astype(BF)
            else:
                g_out[d, s] = (piece + g_in[d, s - 1].astype(F32)).astype(BF)
            go(g_copy(d, s))

    for task in contribution_tasks(1):
        task()
    g_step(0)
    rs_step(1, contribution_tasks(2))
    g_step(1)
    gather_second(att_all, a_ss, a_rs, 0)
    gather_second(att_all, a_ss, a_rs, 1)
    gather_pass(att_all, a_ss, a_rs, 0, 0)
    gather_pass(att_all, a_ss, a_rs, 0, 1)
    gather_near(att_all, a_ss, a_rs, 0)
    rs_step(2, contribution_tasks(3))
    g_step(2)
    gather_pass(att_all, a_ss, a_rs, 1, 0)
    gather_pass(att_all, a_ss, a_rs, 1, 1)
    gather_near(att_all, a_ss, a_rs, 1)
    gather_far(att_all, a_ss, a_rs, 0)
    older = len(sends)
    rs_step(3, contribution_tasks(4))
    g_step(3)
    gather_far(att_all, a_ss, a_rs, 1)
    for copy in sends[:older]:
        copy.wait_send()
    del sends[:older]

    for i in range(2):
        dq_out[i] = (dq[1, i] * SCALE).astype(BF)
    dq_copy = y_copy(5, dq_out, dq_in)
    go(dq_copy)

    gather_end(att_all, a_ss, a_rs)
    wait_w()
    total = nn(att_all[0], w_cols[0])
    for p in range(1, 16):
        total = total + nn(att_all[p], w_cols[p])
    cotm[...] = total.astype(BF)
    for b in range(2):
        mixed_final[b * BLOCK : (b + 1) * BLOCK, :] = in_order(cotm, b)
    put(mixed_final, mixed)

    dq_copy.wait_recv()
    for i in range(2):
        stage[2, i] = (dq[0, i] * SCALE + dq_in[i].astype(F32)).T.astype(BF)
    unsort(2, gq)

    piece = g_piece(7)
    for d in range(2):
        g_copy(d, 3).wait_recv()
        piece = piece + g_in[d, 3].astype(F32)
    gw_final[...] = piece
    put(gw_final, gw)

    for t in range(2):
        for i in range(2):
            for d in range(2):
                rs_copy(d, 3, t, i).wait_recv()
            stage[3 + t, i] = (
                cb[0, 0, t, i] * factors[t]
                + rs_in[0, 3, t, i].astype(F32)
                + rs_in[1, 3, t, i].astype(F32)
            ).astype(BF)
        unsort(3 + t, (gkc, gvc)[t])

    for copy in sends:
        copy.wait_send()
    for store in stores:
        store.wait()


def hand_on(*refs):
    for i in range(7):
        refs[7 + i][...] = refs[i][...]


def per_device(q, kn, vn, kc, vc, w, cot, noise_mask, block_order):
    vmem = pl.BlockSpec(memory_space=pltpu.VMEM)
    smem = pl.BlockSpec(memory_space=pltpu.SMEM)
    rows, width = q.shape
    blk = (BLOCK, HEAD_DIM)
    tblk = (HEAD_DIM, BLOCK)
    dma = pltpu.SemaphoreType.DMA
    narrow = jax.ShapeDtypeStruct((rows, width), BF)
    scratch = [
        *[pltpu.VMEM((rows, width), BF)] * 5,
        pltpu.VMEM(w.shape, BF),
        pltpu.VMEM(cot.shape, BF),
        pltpu.VMEM((2, 2) + blk, BF),
        pltpu.VMEM((2,) + blk, BF),
        pltpu.VMEM((2,) + blk, BF),
        pltpu.VMEM((NZ, 2, 2) + blk, BF),
        pltpu.VMEM((NZ, 2) + tblk, BF),
        pltpu.VMEM((NZ, 2) + tblk, BF),
        pltpu.VMEM((2,) + tblk, BF),
        pltpu.VMEM((2,) + tblk, BF),
        pltpu.VMEM((2, 4, 8, BLOCK), F32),
        pltpu.VMEM((4, 8, BLOCK), F32),
        pltpu.VMEM((2, 2) + tblk, F32),
        pltpu.VMEM((2,) + tblk, BF),
        pltpu.VMEM((2,) + tblk, BF),
        pltpu.VMEM((rows, 256), BF),
        pltpu.VMEM((16, rows, 256), BF),
        pltpu.VMEM((16, HEAD_DIM, 256), BF),
        pltpu.VMEM((4, HEAD_DIM, 512), BF),
        pltpu.VMEM((HEAD_DIM, rows), BF),
        pltpu.VMEM((16, rows, HEAD_DIM), BF),
        pltpu.VMEM((rows, HEAD_DIM), F32),
        pltpu.VMEM((2, 2) + blk, BF),
        pltpu.VMEM((2, 4, 8, BLOCK), F32),
        pltpu.VMEM((2, 2) + tblk, F32),
        pltpu.VMEM((2,) + tblk, BF),
        pltpu.VMEM((2,) + tblk, BF),
        pltpu.VMEM((2, 2, 2, 2) + blk, F32),
        pltpu.VMEM((2, 4, 2, 2) + blk, BF),
        pltpu.VMEM((2, 4, 2, 2) + blk, BF),
        pltpu.VMEM((8, HEAD_DIM, 256), BF),
        pltpu.VMEM((8, HEAD_DIM, 256), BF),
        pltpu.VMEM((2, 4, HEAD_DIM, 256), BF),
        pltpu.VMEM((2, 4, HEAD_DIM, 256), BF),
        pltpu.VMEM((5, 2) + blk, BF),
        pltpu.VMEM((5, rows, width), BF),
        pltpu.VMEM(cot.shape, BF),
        pltpu.VMEM((HEAD_DIM, 256), F32),
        dma((7,)), dma((7,)),
        dma((2, 4, 2, 2)), dma((2, 4, 2, 2)),
        dma((6,)), dma((6,)),
        dma((8,)), dma((8,)),
        dma((22,)), dma((22,)),
        dma((22,)), dma((22,)),
        dma((4,)), dma((4,)),
        dma((14,)), dma((14,)),
        dma((2, 4, 2, 2)), dma((2, 4, 2, 2)),
        dma((2, 4)), dma((2, 4)),
    ]
    shapes = (
        jax.ShapeDtypeStruct(cot.shape, BF),
        narrow, narrow, narrow, narrow, narrow,
        jax.ShapeDtypeStruct((HEAD_DIM, 256), F32),
    )

    outs = pl.pallas_call(
        kernel,
        out_shape=tuple(pltpu.VMEM(shape.shape, shape.dtype) for shape in shapes),
        in_specs=[smem, vmem] + [pl.BlockSpec(memory_space=pltpu.HBM)] * 7,
        scratch_shapes=scratch,
        compiler_params=pltpu.CompilerParams(
            collective_id=0, has_side_effects=True, vmem_limit_bytes=56 * 2**20
        ),
        name="block_attention",
    )(block_order, noise_mask.reshape(4, 128), q, kn, vn, kc, vc, w, cot)
    return pl.pallas_call(
        hand_on,
        out_shape=shapes,
        in_specs=[vmem] * 7,
        out_specs=(vmem,) * 7,
        compiler_params=pltpu.CompilerParams(vmem_limit_bytes=8 * 2**20),
        name="hand_on",
    )(*outs)


def solution(mesh):
    spread = P("ctx", "head")
    return jax.shard_map(
        per_device,
        mesh=mesh,
        in_specs=(spread,) * 5 + (P("head", None), spread, P("ctx"), P()),
        out_specs=(spread,) * 6 + (P("head", "ctx"),),
        check_vma=False,
    )
```

profile of v0, /device:TPU:1, one launch (start us, length us, event | category | flops | bytes accessed | tf_op | source)
XLA Modules:
  0.0 77.1 jit_solution(3112435885009457035)
XLA Ops:
  0.6 75.5 %block_attention.1 = (bf16[512,256]{1,0:T(8,128)(2,1)S(1)}, bf16[512,128]{1,0:T(8,128)(2,1)S(1)}, bf16[512,128]{1,0:T(8,128)(2,1)S(1)}, bf16[512,128]{1,0:T(8,12...) custom-call(s32[32]{0:T(128)} %order.1, s32[4,128]{1,0:T(4,128)} %bitcast.1, ...), custom_call_target="tpu_custom_call" | custom-call | tf_op jit(solution)/shard_map/block_attention/pallas_call | solution.py:697
  76.1 1.0 %hand_on.1 = (bf16[512,256]{1,0:T(8,128)(2,1)}, bf16[512,128]{1,0:T(8,128)(2,1)}, bf16[512,128]{1,0:T(8,128)(2,1)}, bf16[512,128]{1,0:T(8,128)(2,1)}, bf16[512,1...) custom-call(bf16[512,256]{1,0:T(8,128)(2,1)S(1)} %get-tuple-element.14.refs_0_, ...), custom_call_target="tpu_custom_call" | custom-call | tf_op jit(solution)/shard_map/hand_on/pallas_call | solution.py:707
where the time goes:
time: 77.3 us; the launch traced here: 77.1 us
  Pallas kernels  76.5 us (99%)
    pallas_call x1, Pallas kernels, per_device(): pl.pallas_call(kernel, out_shape=tuple((pltpu.VMEM(shape.shape, shape.dty...  75.5 us

commit v1 on v0

--- a/solution.py
+++ b/solution.py
@@ -60,7 +60,7 @@
     mixed, gq, gkn, gvn, gkc, gvc, gw,
     q, kn, vn, kc, vc, w, cot,
     qs, kns, vns, kv, kt, vt, knt, vnt, ml, ml_in, acc, acc_out, acc_in,
-    cotm, cot_all, w_cols, w_mid, att_t, att_all, do_acc, dos, ld, dq, dq_out, dq_in,
+    cotm, cot_all, w_cols, w_mid, att_t, att_all, do_acc, dos, dos_t, ld, dq, dq_out, dq_in,
     cb, rs_out, rs_in, gy_out, gy_in, g_out, g_in, stage, finals, mixed_final, gw_final,
     in_sem, out_sem,
     kv_ss, kv_rs, y_ss, y_rs, gy_ss, gy_rs, c_ss, c_rs, a_ss, a_rs, wm_ss, wm_rs, w_ss, w_rs,
@@ -118,6 +118,93 @@
     for i in range(2):
         kv[z, 0, i] = in_order(kc, i)
         kv[z, 1, i] = in_order(vc, i)
+    pl.semaphore_wait(barrier, 11)
+
+    def kv_chunk(d, s, t, i, slot):
+        chunk = kv.at[slot, t, i]
+        return remote(chunk, chunk, kv_ss.at[d, s - 1, t, i], kv_rs.at[d, s - 1, t, i], z_dev[d])
+
+    def kv_copy(d, s, t, i):
+        return kv_chunk(d, s, t, i, (z + NZ - (s - 1)) % NZ if d == 0 else (z + s - 1) % NZ)
+
+    def kv_wait(d, s, t, i):
+        kv_chunk(d, s, t, i, (z + NZ - s) % NZ if d == 0 else (z + s) % NZ).wait_recv()
+
+    def head_copy(buf, ss, rs, index, slot, dev_head):
+        return remote(buf.at[slot], buf.at[slot], ss.at[index], rs.at[index], (c, dev_head))
+
+    yh_head = head_of(x, 1 - yh, co)
+    sib = head_of(x, yh, 1 - co)
+
+    def x_head(k, yh_, co_):
+        return head_of((x + k) % 4, yh_, co_)
+
+    def rows_at(half):
+        return pl.ds(BLOCK * half, BLOCK)
+
+    def yh_copy(buf, ss, rs, half, slot):
+        chunk = buf.at[slot, rows_at(half)]
+        return remote(chunk, chunk, ss.at[half], rs.at[half], (c, yh_head))
+
+    def x_copy(buf, ss, rs, second, d, kind, slot):
+        index = 2 + 6 * second + 2 * kind + d
+        chunk = buf.at[slot, rows_at(d if kind == 2 else kind)]
+        dev = (c, x_head(1 if d == 0 else 3, yh, co))
+        return remote(chunk, chunk, ss.at[index], rs.at[index], dev)
+
+    def near_slot(second, d):
+        return x_head(3 if d == 0 else 1, 1 - yh if second else yh, co)
+
+    def gather_begin(buf, ss, rs, between=lambda: None):
+        for half in range(2):
+            go(yh_copy(buf, ss, rs, half, h))
+            for d in range(2):
+                go(x_copy(buf, ss, rs, 0, d, half, h))
+            if half == 0:
+                between()
+        go(head_copy(buf, ss, rs, 14, h, sib))
+
+    def gather_second(buf, ss, rs, half):
+        yh_copy(buf, ss, rs, half, yh_head).wait_recv()
+        for d in range(2):
+            go(x_copy(buf, ss, rs, 1, d, half, yh_head))
+        if half:
+            go(head_copy(buf, ss, rs, 15, yh_head, sib))
+
+    def gather_pass(buf, ss, rs, second, d):
+        slot = near_slot(second, d)
+        x_copy(buf, ss, rs, second, d, d, slot).wait_recv()
+        go(x_copy(buf, ss, rs, second, d, 2, slot))
+
+    def gather_near(buf, ss, rs, second):
+        for d in range(2):
+            slot = near_slot(second, d)
+            x_copy(buf, ss, rs, second, d, 1 - d, slot).wait_recv()
+            go(head_copy(buf, ss, rs, 16 + 2 * second + d, slot, sib))
+
+    def gather_far(buf, ss, rs, second):
+        slot = x_head(2, 1 - yh if second else yh, co)
+        for d in range(2):
+            x_copy(buf, ss, rs, second, d, 2, slot).wait_recv()
+        go(head_copy(buf, ss, rs, 20 + second, slot, sib))
+
+    sib_slots = [sib, x_head(0, 1 - yh, 1 - co)]
+    for yh_ in (yh, 1 - yh):
+        sib_slots += [x_head(3, yh_, 1 - co), x_head(1, yh_, 1 - co)]
+    sib_slots += [x_head(2, yh_, 1 - co) for yh_ in (yh, 1 - yh)]
+
+    def gather_end(buf, ss, rs, first=0, last=8):
+        for j in range(first, last):
+            head_copy(buf, ss, rs, 14 + j, sib_slots[j], sib).wait_recv()
+
+    def y_copy(index, src, dst):
+        return remote(src, dst, y_ss.at[index], y_rs.at[index], y_dev)
+
+    for t in range(2):
+        for i in range(2):
+            for d in range(2):
+                go(kv_copy(d, 1, t, i))
+
     loads[2].wait()
     row_id = lax.broadcasted_iota(jnp.int32, (128, 128), 0)
     col_id = lax.broadcasted_iota(jnp.int32, (128, 128), 1)
@@ -132,92 +219,6 @@
     loads[3].wait()
     for i in range(2):
         qs[0, i] = in_order(q, i)
-
-    pl.semaphore_wait(barrier, 11)
-
-    def kv_chunk(d, s, t, i, slot):
-        chunk = kv.at[slot, t, i]
-        return remote(chunk, chunk, kv_ss.at[d, s - 1, t, i], kv_rs.at[d, s - 1, t, i], z_dev[d])
-
-    def kv_copy(d, s, t, i):
-        return kv_chunk(d, s, t, i, (z + NZ - (s - 1)) % NZ if d == 0 else (z + s - 1) % NZ)
-
-    def kv_wait(d, s, t, i):
-        kv_chunk(d, s, t, i, (z + NZ - s) % NZ if d == 0 else (z + s) % NZ).wait_recv()
-
-    def head_copy(buf, ss, rs, index, slot, dev_head):
-        return remote(buf.at[slot], buf.at[slot], ss.at[index], rs.at[index], (c, dev_head))
-
-    yh_head = head_of(x, 1 - yh, co)
-    sib = head_of(x, yh, 1 - co)
-
-    def x_head(k, yh_, co_):
-        return head_of((x + k) % 4, yh_, co_)
-
-    def rows_at(half):
-        return pl.ds(BLOCK * half, BLOCK)
-
-    def yh_copy(buf, ss, rs, half, slot):
-        chunk = buf.at[slot, rows_at(half)]
-        return remote(chunk, chunk, ss.at[half], rs.at[half], (c, yh_head))
-
-    def x_copy(buf, ss, rs, second, d, kind, slot):
-        index = 2 + 6 * second + 2 * kind + d
-        chunk = buf.at[slot, rows_at(d if kind == 2 else kind)]
-        dev = (c, x_head(1 if d == 0 else 3, yh, co))
-        return remote(chunk, chunk, ss.at[index], rs.at[index], dev)
-
-    def near_slot(second, d):
-        return x_head(3 if d == 0 else 1, 1 - yh if second else yh, co)
-
-    def gather_begin(buf, ss, rs, between=lambda: None):
-        for half in range(2):
-            go(yh_copy(buf, ss, rs, half, h))
-            for d in range(2):
-                go(x_copy(buf, ss, rs, 0, d, half, h))
-            if half == 0:
-                between()
-        go(head_copy(buf, ss, rs, 14, h, sib))
-
-    def gather_second(buf, ss, rs, half):
-        yh_copy(buf, ss, rs, half, yh_head).wait_recv()
-        for d in range(2):
-            go(x_copy(buf, ss, rs, 1, d, half, yh_head))
-        if half:
-            go(head_copy(buf, ss, rs, 15, yh_head, sib))
-
-    def gather_pass(buf, ss, rs, second, d):
-        slot = near_slot(second, d)
-        x_copy(buf, ss, rs, second, d, d, slot).wait_recv()
-        go(x_copy(buf, ss, rs, second, d, 2, slot))
-
-    def gather_near(buf, ss, rs, second):
-        for d in range(2):
-            slot = near_slot(second, d)
-            x_copy(buf, ss, rs, second, d, 1 - d, slot).wait_recv()
-            go(head_copy(buf, ss, rs, 16 + 2 * second + d, slot, sib))
-
-    def gather_far(buf, ss, rs, second):
-        slot = x_head(2, 1 - yh if second else yh, co)
-        for d in range(2):
-            x_copy(buf, ss, rs, second, d, 2, slot).wait_recv()
-        go(head_copy(buf, ss, rs, 20 + second, slot, sib))
-
-    def gather_end(buf, ss, rs):
-        slots = [sib, x_head(0, 1 - yh, 1 - co)]
-        for yh_ in (yh, 1 - yh):
-            slots += [x_head(3, yh_, 1 - co), x_head(1, yh_, 1 - co)]
-        slots += [x_head(2, yh_, 1 - co) for yh_ in (yh, 1 - yh)]
-        for j, slot in enumerate(slots):
-            head_copy(buf, ss, rs, 14 + j, slot, sib).wait_recv()
-
-    def y_copy(index, src, dst):
-        return remote(src, dst, y_ss.at[index], y_rs.at[index], y_dev)
-
-    for t in range(2):
-        for i in range(2):
-            for d in range(2):
-                go(kv_copy(d, 1, t, i))
     q_copy = y_copy(0, qs.at[0], qs.at[1])
     gather_begin(cot_all, c_ss, c_rs, lambda: go(q_copy))
 
@@ -306,12 +307,11 @@
                 here = w_cols.at[slot]
                 remote(here, here, w_ss.at[index], w_rs.at[index], dev).wait_recv()
 
-    def add_pieces(core, first):
+    def add_pieces(pieces, first=False):
         for i in range(2):
             rows = slice(i * BLOCK, (i + 1) * BLOCK)
             total = jnp.zeros((BLOCK, HEAD_DIM), F32) if first else do_acc[rows, :]
-            for j in range(8):
-                p = 2 * j + core
+            for p in pieces:
                 columns = pl.ds(pl.multiple_of(p * 256, 256), 256)
                 total = total + nt(cot_all[p, rows], w[:, columns])
             do_acc[rows, :] = total
@@ -345,10 +345,22 @@
         (1, 3): lambda: [gather_pass(*cot_args, 0, d) for d in range(2)],
         (2, 1): lambda: [gather_second(*cot_args, 1), gather_near(*cot_args, 0)],
         (2, 2): lambda: gather_pass(*cot_args, 1, 0),
-        (2, 3): lambda: send_w_across(),
+        (2, 0): lambda: send_w_across(),
         (3, 0): lambda: gather_far(*cot_args, 0),
-        (3, 1): lambda: gather_pass(*cot_args, 1, 1),
+        (3, 1): lambda: [
+            gather_pass(*cot_args, 1, 1),
+            add_pieces([h, near_slot(0, 0), near_slot(0, 1)], True),
+        ],
+        (3, 2): lambda: [
+            gather_end(*cot_args, 0, 2),
+            add_pieces([yh_head, sib_slots[0], sib_slots[1]]),
+        ],
         (3, 3): lambda: gather_near(*cot_args, 1),
+        (4, 0): lambda: [
+            gather_end(*cot_args, 2, 4),
+            add_pieces([x_head(2, yh, co), sib_slots[2], sib_slots[3]]),
+        ],
+        (4, 1): lambda: add_pieces([near_slot(1, 0), near_slot(1, 1)]),
     }
     tasks = []
     for s in range(1, 5):
@@ -377,39 +389,43 @@
     for i in range(2):
         acc_out[i] = acc[1, i].astype(BF)
     ml_copy = y_copy(1, ml.at[1], ml_in)
-    acc_copy = y_copy(2, acc_out, acc_in)
+    acc_copies = [y_copy((2, 6)[i], acc_out.at[i], acc_in.at[i]) for i in range(2)]
     go(ml_copy)
-    go(acc_copy)
+    for copy in acc_copies:
+        go(copy)
     gather_far(*cot_args, 1)
-    add_pieces(co, True)
-    gather_end(*cot_args)
-    add_pieces(1 - co, False)
+    gather_end(*cot_args, 4, 8)
+    add_pieces([x_head(2, 1 - yh, co)] + sib_slots[4:])
     for i in range(2):
         dos[0, i] = do_acc[i * BLOCK : (i + 1) * BLOCK, :].astype(BF)
     do_copy = y_copy(3, dos.at[0], dos.at[1])
     go(do_copy)
     forward_pair(0, (z + 4) % NZ)
-    send_w(0)
-
+
+    for i in range(2):
+        dos_t[i] = dos[0, i].T.astype(F32)
     ml_copy.wait_recv()
-    acc_copy.wait_recv()
-    for i in range(2):
-        own_max, own_sum, own_acc = rows_of(get_state(0, i))
-        other_max, other_sum = ml_in[i][:1], ml_in[2 + i][:1]
+    shares = []
+    for i in range(2):
+        own_max, own_sum, other_max, other_sum = ml[0, i], ml[0, 2 + i], ml_in[i], ml_in[2 + i]
         top = jnp.maximum(own_max, other_max)
         own_part = jnp.exp2((own_max - top) * SCALE2)
         other_part = jnp.exp2((other_max - top) * SCALE2)
         total = own_sum * own_part + other_sum * other_part
-        weighted = own_acc * own_part + acc_in[i].astype(F32) * other_part
-        attended_t = (weighted / total).astype(BF)
+        ld[0, i] = top * SCALE2 + jnp.log2(total)
+        shares.append(((own_part / total)[:1], (other_part / total)[:1]))
+    for i, (own_part, other_part) in enumerate(shares):
+        acc_copies[i].wait_recv()
+        attended_t = (acc[0, i] * own_part + acc_in[i].astype(F32) * other_part).astype(BF)
         att_t[:, i * BLOCK : (i + 1) * BLOCK] = attended_t
-        att_all[h, i * BLOCK : (i + 1) * BLOCK, :] = attended_t.T
-        grads_t = dos[0, i].T.astype(F32)
-        row_dot = jnp.sum(grads_t * attended_t.astype(F32), axis=0, keepdims=True)
-        ld[0, i] = jnp.broadcast_to(top * SCALE2 + jnp.log2(total), (8, BLOCK))
+        row_dot = jnp.sum(dos_t[i] * attended_t.astype(F32), axis=0, keepdims=True)
         ld[0, 2 + i] = jnp.broadcast_to(row_dot, (8, BLOCK))
     ld_copy = y_copy(4, ld.at[0], ld.at[1])
     go(ld_copy)
+    send_w(0)
+    for i in range(2):
+        rows = slice(i * BLOCK, (i + 1) * BLOCK)
+        att_all[h, rows, :] = att_t[:, rows].T
     gather_begin(att_all, a_ss, a_rs)
 
     def gy_slot(j):
@@ -600,13 +616,6 @@
         stage[2, i] = (dq[0, i] * SCALE + dq_in[i].astype(F32)).T.astype(BF)
     unsort(2, gq)
 
-    piece = g_piece(7)
-    for d in range(2):
-        g_copy(d, 3).wait_recv()
-        piece = piece + g_in[d, 3].astype(F32)
-    gw_final[...] = piece
-    put(gw_final, gw)
-
     for t in range(2):
         for i in range(2):
             for d in range(2):
@@ -617,6 +626,13 @@
                 + rs_in[1, 3, t, i].astype(F32)
             ).astype(BF)
         unsort(3 + t, (gkc, gvc)[t])
+
+    piece = g_piece(7)
+    for d in range(2):
+        g_copy(d, 3).wait_recv()
+        piece = piece + g_in[d, 3].astype(F32)
+    gw_final[...] = piece
+    put(gw_final, gw)
 
     for copy in sends:
         copy.wait_send()
@@ -662,6 +678,7 @@
         pltpu.VMEM((16, rows, HEAD_DIM), BF),
         pltpu.VMEM((rows, HEAD_DIM), F32),
         pltpu.VMEM((2, 2) + blk, BF),
+        pltpu.VMEM((2,) + tblk, F32),
         pltpu.VMEM((2, 4, 8, BLOCK), F32),
         pltpu.VMEM((2, 2) + tblk, F32),
         pltpu.VMEM((2,) + tblk, BF),
@@ -679,7 +696,7 @@
         pltpu.VMEM((HEAD_DIM, 256), F32),
         dma((7,)), dma((7,)),
         dma((2, 4, 2, 2)), dma((2, 4, 2, 2)),
-        dma((6,)), dma((6,)),
+        dma((7,)), dma((7,)),
         dma((8,)), dma((8,)),
         dma((22,)), dma((22,)),
         dma((22,)), dma((22,)),

time: 77.3 us -> 76.2 us (0.986)
  Pallas kernels: 76.5 us -> 75.4 us
    pallas_call x1, Pallas kernels: 75.5 us -> 74.4 us  [per_device(): pl.pallas_call(kernel, out_shape=tuple((pltpu.VMEM(shape.shape, shape.dty...]
where the time goes in v1:
time: 76.2 us; the launch traced here: 76.1 us
  Pallas kernels  75.4 us (99%)
    pallas_call x1, Pallas kernels, per_device(): pl.pallas_call(kernel, out_shape=tuple((pltpu.VMEM(shape.shape, shape.dty...  74.4 us

profile of v1, /device:TPU:1, one launch (start us, length us, event | category | flops | bytes accessed | tf_op | source)
XLA Modules:
  0.0 76.1 jit_solution(11906419106504430359)
XLA Ops:
  0.6 74.4 %block_attention.1 = (bf16[512,256]{1,0:T(8,128)(2,1)S(1)}, bf16[512,128]{1,0:T(8,128)(2,1)S(1)}, bf16[512,128]{1,0:T(8,128)(2,1)S(1)}, bf16[512,128]{1,0:T(8,12...) custom-call(s32[32]{0:T(128)} %order.1, s32[4,128]{1,0:T(4,128)} %bitcast.1, ...), custom_call_target="tpu_custom_call" | custom-call | tf_op jit(solution)/shard_map/block_attention/pallas_call | solution.py:714
  75.1 1.0 %hand_on.1 = (bf16[512,256]{1,0:T(8,128)(2,1)}, bf16[512,128]{1,0:T(8,128)(2,1)}, bf16[512,128]{1,0:T(8,128)(2,1)}, bf16[512,128]{1,0:T(8,128)(2,1)}, bf16[512,1...) custom-call(bf16[512,256]{1,0:T(8,128)(2,1)S(1)} %get-tuple-element.14.refs_0_, ...), custom_call_target="tpu_custom_call" | custom-call | tf_op jit(solution)/shard_map/hand_on/pallas_call | solution.py:724
